TPU v7x, 32 devices: a whole 2x2x4 slice. The times are simulated.
32 devices in a mesh: groups: 2 (over y), seq: 4 (over z), chan: 2 (over x), dp: 2 (over core).
Axes of the slice: x: 2, y: 2, z: 4, core: 2. Of those that a mesh axis runs over, the one named last changes fastest.
Arguments:
- conv_input: bfloat16 [4, 2048, 2048], P(('groups', 'dp'), 'seq', 'chan'), parts along dimension 0, may hold values from -6 to 6
- conv_weight: float32 [4, 2048], P(None, 'chan'), may hold values from -3 to 3
- log_decay: float32 [4, 2048, 32], P(('groups', 'dp'), 'seq', 'chan'), parts along dimension 0, as said below
- state_in: bfloat16 [4, 2048, 128], P(('groups', 'dp'), 'seq'), parts along dimension 0, may hold values from -1.5 to 1.5
- state_out: bfloat16 [4, 2048, 128], P(('groups', 'dp'), 'seq'), parts along dimension 0, may hold values from -1.5 to 1.5
- out_grad: bfloat16 [4, 2048, 2048], P(('groups', 'dp'), 'seq', 'chan'), parts along dimension 0, may hold values from -3 to 3
- lengths: int32 [4], P(('groups', 'dp')), parts along dimension 0, may hold values from 1 to 2048, as said below
- segment_starts: int32 [4, 2], P(('groups', 'dp')), parts along dimension 0, may hold values from 1 to 2047
Outputs:
- input_grad: bfloat16 [4, 2048, 2048], P(('groups', 'dp'), 'seq', 'chan'), parts along dimension 0
- state_in_grad: float32 [4, 2048, 128], P(('groups', 'dp'), 'seq'), parts along dimension 0
- state_out_grad: float32 [4, 2048, 128], P(('groups', 'dp'), 'seq'), parts along dimension 0
- weight_grad: float32 [8, 2048], P('groups', 'chan'), parts along dimension 0
There are 2 independent parts, one for each index of `groups`. A program takes and returns all parts, laid end to end along the dimension named above; an argument that names none is the same for every part. Nothing has to cross between parts.
Inputs may be any that keep to these rules, and one draw needn't show every extreme that they name: `lengths`: at least one series of a group runs the full 2048 steps. `log_decay`: strictly negative.
All inputs are finite; a program needn't handle non-finite values.
Results may differ from a plain program's by a relative error of at most 0.019.
Values may be sent and summed in bfloat16 or wider, within the bound.
A program may use at most 128 MiB of HBM per device.

v0:
```python
import math
import jax
import jax.numpy as jnp
from jax import lax
from jax.sharding import PartitionSpec as P

BLOCK = 256


def shifted(block, axis, distance):
    devices = range(lax.axis_size(axis))
    route = [(i - distance, i) for i in devices if i - distance in devices]
    return lax.ppermute(block, axis, route)


def prefix(part, axis, combine, identity, reverse):
    count = lax.axis_size(axis)
    place = lax.axis_index(axis)
    ahead = count - 1 - place if reverse else place
    gathered = jax.tree.map(lambda a: lax.all_gather(a, axis), part)
    state = jax.tree.map(lambda a, e: jnp.zeros_like(a) + jnp.asarray(e, a.dtype), part, identity)

    def one(hop, state):
        source = count - 1 - hop if reverse else hop
        return combine(
            state, jax.tree.map(lambda a: lax.dynamic_index_in_dim(a, source, 0, False), gathered)
        )

    return lax.fori_loop(0, ahead, one, state)


def block_decay(logs, resets):
    kept = jnp.where(resets[:, :, None], jnp.float32(0.0), logs)
    running = jnp.cumsum(kept, axis=1)
    segment = jnp.cumsum(resets.astype(jnp.int32), axis=1)
    steps = logs.shape[1]
    order = jnp.arange(steps, dtype=jnp.int32)
    final = running[:, -1:, :]
    final_seg = segment[:, -1:]
    start_decay = jnp.where((segment == 0)[:, :, None], jnp.exp(running), jnp.float32(0.0))
    end_decay = jnp.where(
        (segment == final_seg)[:, :, None], jnp.exp(final - running), jnp.float32(0.0)
    )
    whole = jnp.where(final_seg == 0, jnp.exp(final[:, 0, :]), jnp.float32(0.0))
    per_head = jnp.transpose(running, (0, 2, 1))
    spread = per_head[:, :, :, None] - per_head[:, :, None, :]
    linked = (segment[:, :, None] == segment[:, None, :]) & (order[:, None] >= order[None, :])[None]
    linked = linked[:, None]
    decay_map = jnp.where(
        linked, jnp.exp(jnp.where(linked, spread, jnp.float32(0.0))), jnp.float32(0.0)
    )
    return (decay_map, start_decay, end_decay, whole)


def split_pair(values):
    upper = values.astype(jnp.bfloat16)
    lower = (values - upper.astype(jnp.float32)).astype(jnp.bfloat16)
    return (upper, lower)


def pair_product(form, left, right):
    upper, lower = left
    return jnp.einsum(form, upper, right, preferred_element_type=jnp.float32) + jnp.einsum(
        form, lower, right, preferred_element_type=jnp.float32
    )


def block_state(values, matrix, decay):
    scaled = decay[..., None] * values.astype(jnp.float32)
    return pair_product("bshp,bsn->bhpn", split_pair(scaled), matrix)


def compose(earlier, later):
    return (earlier[0] * later[0], later[0][:, :, None, None] * earlier[1] + later[1])


def block_outputs(
    scan_in, masked, in_mat, out_mat, decay_map, start_decay, end_decay, state, grad_state
):
    scores = jnp.einsum("bthp,bshp->bhts", masked, scan_in, preferred_element_type=jnp.float32)
    weighted = (scores * decay_map).astype(jnp.bfloat16)
    inner = jnp.einsum("btn,bsn->bts", out_mat, in_mat, preferred_element_type=jnp.float32)
    carried = (inner[:, None] * decay_map).astype(jnp.bfloat16)
    scaled_grads = start_decay[..., None] * masked.astype(jnp.float32)
    scaled_scan = end_decay[..., None] * scan_in.astype(jnp.float32)
    state_pair = split_pair(state)
    grad_pair = split_pair(grad_state)
    out_part = jnp.einsum("bhts,bsn->btn", weighted, in_mat, preferred_element_type=jnp.float32)
    out_part = out_part + pair_product("bthp,bhpn->btn", split_pair(scaled_grads), state_pair[0])
    out_part = out_part + pair_product("bthp,bhpn->btn", split_pair(scaled_grads), state_pair[1])
    in_part = jnp.einsum("bhrt,brn->btn", weighted, out_mat, preferred_element_type=jnp.float32)
    in_part = in_part + pair_product("bthp,bhpn->btn", split_pair(scaled_scan), grad_pair[0])
    in_part = in_part + pair_product("bthp,bhpn->btn", split_pair(scaled_scan), grad_pair[1])
    scan_grad = jnp.einsum("bhrt,brhp->bthp", carried, masked, preferred_element_type=jnp.float32)
    scan_grad = scan_grad + end_decay[..., None] * pair_product("bhpn,btn->bthp", grad_pair, in_mat)
    return (out_part, in_part, scan_grad)


def backward_conv(padded, weights, count):
    kernel = weights.shape[0]
    summed = jnp.zeros((padded.shape[0], count, padded.shape[2]), jnp.float32)
    for offset in range(kernel):
        start = kernel - 1 - offset
        summed = summed + weights[offset] * padded[:, start : start + count].astype(jnp.float32)
    return summed.astype(jnp.bfloat16)


def per_device(
    conv_input, conv_weight, log_decay, state_in, state_out, out_grad, lengths, segment_starts
):
    batch, local, channels = conv_input.shape
    heads = log_decay.shape[2]
    width = channels // heads
    states = state_in.shape[2]
    kernel = conv_weight.shape[0]
    seq_count = lax.axis_size("seq")
    seq_index = lax.axis_index("seq")
    rim = shifted(conv_input[:, local - (kernel - 1) :, :], "seq", 1)
    padded = jnp.concatenate([rim, conv_input], axis=1)
    mixed = jnp.zeros((batch, local, channels), jnp.float32)
    for offset in range(kernel):
        mixed = mixed + conv_weight[offset] * padded[:, offset : offset + local].astype(jnp.float32)
    position = seq_index * local + jnp.arange(local, dtype=jnp.int32)
    valid = (position[None, :] < lengths[:, None])[:, :, None]
    resets = jnp.any(segment_starts[:, None, :] == position[None, :, None], axis=2)
    gain = jnp.where(resets[:, :, None], jnp.float32(1.0), jnp.sqrt(-jnp.expm1(2.0 * log_decay)))
    sigmoid_u = jax.nn.sigmoid(mixed)
    activated = ((mixed * sigmoid_u).reshape(batch, local, heads, width) * gain[..., None]).reshape(
        batch, local, channels
    )
    scan_in = (
        jnp.where(valid, activated, jnp.float32(0.0))
        .astype(jnp.bfloat16)
        .reshape(batch, local, heads, width)
    )
    masked = jnp.where(valid, out_grad, jnp.zeros_like(out_grad)).reshape(
        batch, local, heads, width
    )
    count = local // BLOCK
    records = []
    carried_decay = jnp.ones((batch, heads), jnp.float32)
    forward_sum = jnp.zeros((batch, heads, width, states), jnp.float32)
    backward_sum = jnp.zeros((batch, heads, width, states), jnp.float32)
    for index in range(count):
        span = slice(index * BLOCK, (index + 1) * BLOCK)
        decay_map, start_decay, end_decay, whole = block_decay(log_decay[:, span], resets[:, span])
        pushed = block_state(scan_in[:, span], state_in[:, span], end_decay)
        pulled = block_state(masked[:, span], state_out[:, span], start_decay)
        records.append((span, decay_map, start_decay, end_decay, whole, pushed, pulled))
        forward_sum = whole[:, :, None, None] * forward_sum + pushed
        carried_decay = carried_decay * whole
    for record in reversed(records):
        backward_sum = record[4][:, :, None, None] * backward_sum + record[6]
    identity = (jnp.ones_like(carried_decay), jnp.zeros_like(forward_sum))
    _, entering = prefix((carried_decay, forward_sum), "seq", compose, identity, False)
    _, leaving = prefix((carried_decay, backward_sum), "seq", compose, identity, True)
    state_now = entering
    entries = []
    for record in records:
        entries.append(state_now)
        state_now = record[4][:, :, None, None] * state_now + record[5]
    grad_now = leaving
    exits = [grad_now] * count
    for index in reversed(range(count)):
        exits[index] = grad_now
        grad_now = records[index][4][:, :, None, None] * grad_now + records[index][6]
    out_list = []
    in_list = []
    scan_list = []
    for index in range(count):
        span, decay_map, start_decay, end_decay, whole, pushed, pulled = records[index]
        out_part, in_part, scan_grad = block_outputs(
            scan_in[:, span],
            masked[:, span],
            state_in[:, span],
            state_out[:, span],
            decay_map,
            start_decay,
            end_decay,
            entries[index],
            exits[index],
        )
        out_list.append(out_part)
        in_list.append(in_part)
        scan_list.append(scan_grad)
    out_local = jnp.concatenate(out_list, axis=1)
    in_local = jnp.concatenate(in_list, axis=1)
    scan_grad = jnp.concatenate(scan_list, axis=1)
    state_in_grad, state_out_grad = (
        lax.psum(in_local.astype(jnp.bfloat16), "chan").astype(jnp.float32),
        lax.psum(out_local.astype(jnp.bfloat16), "chan").astype(jnp.float32),
    )
    slope = sigmoid_u * (1.0 + mixed * (1.0 - sigmoid_u))
    mixed_grad = (scan_grad * gain[..., None]).reshape(batch, local, channels) * slope
    mixed_grad = jnp.where(valid, mixed_grad, jnp.float32(0.0)).astype(jnp.bfloat16)
    after = shifted(mixed_grad[:, : kernel - 1, :], "seq", -1)
    input_grad = backward_conv(jnp.concatenate([mixed_grad, after], axis=1), conv_weight, local)
    wide_grad = mixed_grad.astype(jnp.float32)
    rows = []
    for offset in range(kernel):
        rows.append(
            jnp.sum(wide_grad * padded[:, offset : offset + local].astype(jnp.float32), axis=(0, 1))
        )
    factor = 1.0 / math.sqrt(batch * lax.axis_size("dp") * local * seq_count)
    weight_grad = lax.psum(jnp.stack(rows) * factor, ("seq", "dp"))
    return (input_grad, state_in_grad, state_out_grad, weight_grad)


def solution(mesh):
    placed = (
        P(("groups", "dp"), "seq", "chan"),
        P(None, "chan"),
        P(("groups", "dp"), "seq", "chan"),
        P(("groups", "dp"), "seq", None),
        P(("groups", "dp"), "seq", None),
        P(("groups", "dp"), "seq", "chan"),
        P(("groups", "dp")),
        P(("groups", "dp"), None),
    )
    return jax.shard_map(
        per_device,
        mesh=mesh,
        in_specs=placed,
        out_specs=(
            P(("groups", "dp"), "seq", "chan"),
            P(("groups", "dp"), "seq", None),
            P(("groups", "dp"), "seq", None),
            P("groups", "chan"),
        ),
        check_vma=False,
    )
```

profile of v0, /device:TPU:0, one launch (start us, length us, event | category | flops | bytes accessed | tf_op | source)
XLA Modules:
  0.0 183.1 jit_solution(17551655215464907712)
XLA Ops:
  18.6 1.5 copy.104
  25.3 5.6 %collective-permute-start = (bf16[1,3,1024]{1,2,0:T(8,128)(2,1)}, bf16[1,3,1024]{1,2,0:T(8,128)(2,1)}, u32[]{:S(2)}, u32[]{:S(2)}) collective-permute-start(bf16[1,3,1024]{1,2,0:T(8,128)(2,1)} %copy.122), channel_id=1, source_target_pairs={{0,4},{4,8},{8,12},{1,5},{5,9},{9,13},{2,6},{6,10},{10,14},{3,7},{... | collective-permute-start | bytes 18440 | tf_op jit(solution)/shard_map/ppermute | solution.py:13
  31.0 1.5 copy.123
  32.9 13.7 %all_gather.18 = f32[4,1,16]{2,1,0:T(1,128)} all-gather(f32[1,1,16]{2,1,0:T(1,128)S(1)} %mul.350), channel_id=1, replica_groups=mesh['groups'=2,'seq'=4,'chan'=2,'dp'=2] {'seq'}, dimensions={0}, use_global_device_ids=true | all-gather | bytes 320 | tf_op jit(solution)/shard_map/all_gather | solution.py:20
  51.1 21.5 %all-gather.5.cloned.1.call-done = f32[64,64,128]{2,1,0:T(8,128)} async-done(((f32[16,64,128]{2,1,0:T(8,128)}), f32[64,64,128]{2,1,0:T(8,128)}) %all-gather.5.cloned.1.call-update) | async-done | bytes 2097168 | tf_op jit(solution)/shard_map/all_gather | solution.py:20
  72.6 5.5 %while.26 = (s32[]{:T(128)}, f32[1,16,64,128]{3,2,1,0:T(8,128)S(1)}, s32[]{:T(128)}, f32[4,1,16]{2,1,0:T(1,128)}, f32[4,1,16,64,128]{4,3,2,1,0:T(8,128)}, /*index=5*/s32[]{:T(128)}, s32[]{:T(128)}, s32[]{:T(128)}, s32[]{:T(128)}) while((s32[]{:T(128)}, f32[1,16,64,128]{3,2,1,0:T(8,128)S(1)}, s32[]{:T(128)}, f32[4,1,16]{2,1,0:T(1,128)}, ...), condition=%wide.region_10.11_spmd, body=%wide.region_9.10_spmd.sunk | while | flops 262150 | bytes 1573203 | solution.py:29
  73.2 1.2 bitcast_add_fusion.12
  75.0 1.2 bitcast_add_fusion.12
  76.9 1.2 bitcast_add_fusion.12
  79.8 1.3 fusion.34
  81.2 1.3 fusion.35
  82.6 6.2 %fusion.12 = (f32[1024]{0:T(1024)S(1)}, f32[1024]{0:T(1024)S(1)}, f32[1024]{0:T(1024)S(1)}, f32[1024]{0:T(1024)S(1)}, bf16[1,512,1024]{1,2,0:T(8,128)(2,1)}, /*index=5*/f32[1,512,1024]{1,2,0:T(8,128)S(1)}) fusion(bf16[1,512,1024]{1,2,0:T(8,128)(2,1)S(1)} %copy.123, bf16[1,3,1024]{1,2,0:T(8,128)(2,1)} %collective-permute-done, ...), kind=kLoop, calls=%fused_computation.35 | loop fusion | flops 25686016 | bytes 6363648 | tf_op jit(solution)/shard_map/reduce_sum | solution.py:202
  91.7 1.7 slice.175
  93.3 1.3 collective-permute-start.1
  94.7 40.0 %psum.23 = f32[4,1024]{1,0:T(4,128)} all-reduce(f32[4,1024]{1,0:T(4,128)S(1)} %maximum_multiply_fusion), channel_id=1, replica_groups=mesh['groups'=2,'seq'=4,'chan'=2,'dp'=2] {'seq','dp'}, use_global_device_ids=true, to_apply=%region_21.22 | all-reduce | flops 4096 | bytes 32768 | tf_op jit(solution)/shard_map/psum | solution.py:205
  134.6 1.4 convolution_bitcast_fusion.14
  136.1 1.6 convolution_bitcast_fusion.12
  138.4 1.6 convert_reduce_fusion.1
  141.7 1.6 convert_reduce_fusion
  149.2 3.9 %fusion.11 = bf16[1,512,1024]{1,2,0:T(8,128)(2,1)S(1)} fusion(bf16[1,512,1024]{1,2,0:T(8,128)(2,1)S(1)} %copy-done, bf16[1,3,1024]{1,2,0:T(8,128)(2,1)} %collective-permute-done.1, f32[1024]{0:T(1024)S(1)} %bitcast.442, f32[1024]{0:T(1024)S(1)} %bitcast.444, f32[1024]{0:T(1024)S(1)} %bitcast.440, f32[1024]{0:T(1024)S(1)} %bitcast.438), kind=kLoop, calls=%fused_computation.34 | loop fusion | flops 11010048 | bytes 2119680 | tf_op jit(solution)/shard_map/convert_element_type | solution.py:105
  153.1 1.3 copy.126
  154.4 19.0 %all-reduce.3.cloned.1.call-done = (bf16[1,512,128]{2,1,0:T(8,128)(2,1)}, bf16[1,512,128]{2,1,0:T(8,128)(2,1)}) async-done(((bf16[1,512,128]{2,1,0:T(8,128)(2,1)}, bf16[1,512,128]{2,1,0:T(8,128)(2,1)}), (bf16[1,512,128]{2,1,0:T(8,128)(2,1)}, bf16[1,512,128]{2,1,0:T(8,128)(2,1)})) %all-reduce.3.cloned.1.call-update) | async-done | bytes 262160 | tf_op jit(solution)/shard_map/psum | solution.py:190
  173.3 1.6 convert_element_type.247
  175.0 1.6 convert_element_type.254
  (208 shorter events, 32.2 us)
Async XLA Ops:
  7.2 65.4 %all-gather.5.cloned.1.call-start = ((), (), s32[]{:S(2)}) async-start(), calls=%async_computation | async-start | bytes 2621440 | tf_op jit(solution)/shard_map/all_gather | solution.py:20
  13.6 4.9 %copy-start.31 = (s32[256]{0:T(256)}, s32[256]{0:T(256)S(1)}, u32[]{:S(2)}) copy-start(s32[256]{0:T(256)S(1)} %get-tuple-element.233) | copy-start | bytes 3076
  17.9 2.7 %copy-start.9 = (f32[1,256,16]{1,2,0:T(8,128)}, f32[1,256,16]{1,2,0:T(8,128)S(1)}, u32[]{:S(2)}) copy-start(f32[1,256,16]{1,2,0:T(8,128)S(1)} %copy.155) | copy-start | bytes 49156
  18.6 1.6 copy-start.41
  23.6 23.0 %copy-start.30 = (f32[4,1024]{1,0:T(4,128)S(1)}, f32[4,1024]{1,0:T(4,128)}, u32[]{:S(2)}) copy-start(f32[4,1024]{1,0:T(4,128)} %param.13) | copy-start | bytes 49156
  23.6 24.8 %copy-start.13 = (f32[1,512,16]{1,2,0:T(8,128)S(1)}, f32[1,512,16]{1,2,0:T(8,128)}, u32[]{:S(2)}) copy-start(f32[1,512,16]{1,2,0:T(8,128)} %param.14) | copy-start | bytes 98308
  23.6 24.8 %copy-start.36 = (pred[512]{0:T(512)(128)(4,1)S(1)}, pred[512]{0:T(512)(128)(4,1)}, u32[]{:S(2)}) copy-start(pred[512]{0:T(512)(128)(4,1)} %copy-done.35) | copy-start | bytes 1540
  23.6 24.8 %copy-start.32 = (s32[256]{0:T(256)S(1)}, s32[256]{0:T(256)}, u32[]{:S(2)}) copy-start(s32[256]{0:T(256)} %copy-done.31) | copy-start | bytes 3076
  23.6 25.6 %copy-start.34 = (s32[256]{0:T(256)S(1)}, s32[256]{0:T(256)}, u32[]{:S(2)}) copy-start(s32[256]{0:T(256)} %copy-done.33) | copy-start | bytes 3076
  23.6 25.7 %copy-start.3 = (bf16[1,512,128]{2,1,0:T(8,128)(2,1)S(1)}, bf16[1,512,128]{2,1,0:T(8,128)(2,1)}, u32[]{:S(2)}) copy-start(bf16[1,512,128]{2,1,0:T(8,128)(2,1)} %param.15) | copy-start | bytes 393220
  23.6 120.6 %all-gather.7.cloned.1.call-start = ((), (), s32[]{:S(2)}) async-start(), calls=%async_computation.1 | async-start | bytes 2621440 | tf_op jit(solution)/shard_map/all_gather | solution.py:20
  25.3 57.2 %collective-permute-start = (bf16[1,3,1024]{1,2,0:T(8,128)(2,1)}, bf16[1,3,1024]{1,2,0:T(8,128)(2,1)}, u32[]{:S(2)}, u32[]{:S(2)}) collective-permute-start(bf16[1,3,1024]{1,2,0:T(8,128)(2,1)} %copy.122), channel_id=1, source_target_pairs={{0,4},{4,8},{8,12},{1,5},{5,9},{9,13},{2,6},{6,10},{10,14},{3,7},{... | collective-permute-start | bytes 18440 | tf_op jit(solution)/shard_map/ppermute | solution.py:13
  49.3 31.9 %copy-start.14 = (pred[256,256]{1,0:T(8,128)(4,1)}, pred[256,256]{1,0:T(8,128)(4,1)S(1)}, u32[]{:S(2)}) copy-start(pred[256,256]{1,0:T(8,128)(4,1)S(1)} %fusion.110) | copy-start | bytes 196612
  72.6 5.8 %copy-start.39 = (f32[16]{0:T(128)S(1)}, f32[16]{0:T(128)}, u32[]{:S(2)}) copy-start(f32[16]{0:T(128)} %get-tuple-element.255) | copy-start | bytes 196
  91.6 81.7 %all-reduce.3.cloned.1.call-start = ((), (), s32[]{:S(2)}) async-start(), calls=%async_computation.2 | async-start | bytes 524288 | tf_op jit(solution)/shard_map/psum | solution.py:190
  93.3 55.8 %collective-permute-start.1 = (bf16[1,3,1024]{1,2,0:T(8,128)(2,1)}, bf16[1,3,1024]{1,2,0:T(8,128)(2,1)}, u32[]{:S(2)}, u32[]{:S(2)}) collective-permute-start(bf16[1,3,1024]{1,2,0:T(8,128)(2,1)} %slice.175), channel_id=1, source_target_pairs={{4,0},{8,4},{12,8},{5,1},{9,5},{13,9},{6,2},{10,6},{14,10},{7,3},{... | collective-permute-start | bytes 18440 | tf_op jit(solution)/shard_map/ppermute | solution.py:13
  134.6 3.1 %copy-start.2 = (f32[1,16,64,128]{3,2,1,0:T(8,128)S(1)}, f32[1,16,64,128]{3,2,1,0:T(8,128)}, u32[]{:S(2)}) copy-start(f32[1,16,64,128]{3,2,1,0:T(8,128)} %copy-done.1) | copy-start | bytes 1572868
  136.1 2.3 %copy-start.17 = (pred[256,256]{1,0:T(8,128)(4,1)S(1)}, pred[256,256]{1,0:T(8,128)(4,1)}, u32[]{:S(2)}) copy-start(pred[256,256]{1,0:T(8,128)(4,1)} %fusion.111) | copy-start | bytes 196612
  136.1 2.3 %copy-start.29 = (f32[16,256]{1,0:T(8,128)S(1)}, f32[16,256]{1,0:T(8,128)}, u32[]{:S(2)}) copy-start(f32[16,256]{1,0:T(8,128)} %bitcast_add_fusion.5) | copy-start | bytes 49156
  147.3 1.8 copy-start
  147.3 1.8 copy-start.19
  147.3 1.8 copy-start.21
  147.3 1.8 copy-start.23
  147.3 1.8 copy-start.25
  (25 other events, 28.1 us)
Sparse Core Ops, SparseCore 0:
  23.7 48.7 all-gather.4
  91.7 46.4 all-gather.6
  149.2 24.0 all-reduce.2
where the time goes:
time: 184 us; the launch traced here: 183 us
  blocking collectives  53.6 us (29%)
  waiting for transfers between devices  40.5 us (22%)
  other arithmetic  26.6 us (14%)
  matrix products  21.6 us (12%)
  between operations  18 us (10%)
  local copies, waits for them, and re-layouts  15.7 us (9%)
  starting transfers between devices  7.02 us (4%)
    psum x1, blocking collectives, per_device(): weight_grad = lax.psum(jnp.stack(rows) * factor, ('seq', 'dp'))  40 us
    all_gather x2, waiting for transfers between devices, prefix(): gathered = jax.tree.map(lambda a: lax.all_gather(a, axis), part)  21.5 us
    psum x1, waiting for transfers between devices, per_device(): lax.psum(in_local.astype(jnp.bfloat16), 'chan').astype(jnp.float32)  19 us
    all_gather x1, blocking collectives, prefix(): gathered = jax.tree.map(lambda a: lax.all_gather(a, axis), part)  13.7 us
    dot_general x14, matrix products, pair_product(): jnp.einsum(form, lower, right, preferred_element_type=jnp.float32)  8.56 us
    ppermute x2, starting transfers between devices, shifted(): return lax.ppermute(block, axis, route)  6.9 us
    reduce_sum x1, other arithmetic, per_device(): jnp.sum(wide_grad * padded[:, offset:offset + local].astype(jnp.float32),...  6.22 us
    unnamed x95, local copies, waits for them, and re-layouts  6.05 us
  transfers between devices with their start and end apart: 5, of which 2 were waited for; matrix products, arithmetic and copies ran while one was open for 21% of the time, Pallas kernels for 0%

commit v1 on v0

--- a/solution.py
+++ b/solution.py
@@ -202,7 +202,7 @@
             jnp.sum(wide_grad * padded[:, offset : offset + local].astype(jnp.float32), axis=(0, 1))
         )
     factor = 1.0 / math.sqrt(batch * lax.axis_size("dp") * local * seq_count)
-    weight_grad = lax.psum(jnp.stack(rows) * factor, ("seq", "dp"))
+    weight_grad = jnp.sum(lax.all_gather(jnp.stack(rows) * factor, ("seq", "dp")), axis=0)
     return (input_grad, state_in_grad, state_out_grad, weight_grad)
 
 

time: 184 us -> 179 us (0.973)
  blocking collectives: 53.6 us -> 41.3 us
  waiting for transfers between devices: 40.5 us -> 47.2 us
    psum x1 -> x0, blocking collectives: 40 us -> none  [per_device(): weight_grad = lax.psum(jnp.stack(rows) * factor, ('seq', 'dp'))]
    all_gather x0 -> x1, blocking collectives: none -> 27.7 us  [per_device(): lax.all_gather(jnp.stack(rows) * factor, ('seq', 'dp'))]
    all_gather x2, waiting for transfers between devices: 21.5 us -> 27.4 us  [prefix(): gathered = jax.tree.map(lambda a: lax.all_gather(a, axis), part)]
    unnamed x95 -> x99, local copies, waits for them, and re-layouts: 6.05 us -> 6.05 us
  transfers between devices with their start and end apart: 5 -> 5, of which waited for: 2 -> 3; matrix products, arithmetic and copies ran while one was open for 21% -> 21% of each run, Pallas kernels for 0% -> 0%
where the time goes in v1:
time: 179 us; the launch traced here: 178 us
  waiting for transfers between devices  47.2 us (26%)
  blocking collectives  41.3 us (23%)
  other arithmetic  27.2 us (15%)
  matrix products  21.6 us (12%)
  between operations  18 us (10%)
  local copies, waits for them, and re-layouts  15.6 us (9%)
  starting transfers between devices  7.04 us (4%)
    all_gather x1, blocking collectives, per_device(): lax.all_gather(jnp.stack(rows) * factor, ('seq', 'dp'))  27.7 us
    all_gather x2, waiting for transfers between devices, prefix(): gathered = jax.tree.map(lambda a: lax.all_gather(a, axis), part)  27.4 us
    psum x1, waiting for transfers between devices, per_device(): lax.psum(in_local.astype(jnp.bfloat16), 'chan').astype(jnp.float32)  19.8 us
    all_gather x1, blocking collectives, prefix(): gathered = jax.tree.map(lambda a: lax.all_gather(a, axis), part)  13.7 us
    dot_general x14, matrix products, pair_product(): jnp.einsum(form, lower, right, preferred_element_type=jnp.float32)  8.59 us
    ppermute x2, starting transfers between devices, shifted(): return lax.ppermute(block, axis, route)  6.92 us
    reduce_sum x1, other arithmetic, per_device(): jnp.sum(wide_grad * padded[:, offset:offset + local].astype(jnp.float32),...  6.22 us
    unnamed x99, local copies, waits for them, and re-layouts  6.05 us
  transfers between devices with their start and end apart: 5, of which 3 were waited for; matrix products, arithmetic and copies ran while one was open for 21% of the time, Pallas kernels for 0%

profile of v1, /device:TPU:0, one launch (start us, length us, event | category | flops | bytes accessed | tf_op | source)
XLA Modules:
  0.0 178.2 jit_solution(10396637352771961481)
XLA Ops:
  18.6 1.5 copy.104
  25.3 5.6 %collective-permute-start = (bf16[1,3,1024]{1,2,0:T(8,128)(2,1)}, bf16[1,3,1024]{1,2,0:T(8,128)(2,1)}, u32[]{:S(2)}, u32[]{:S(2)}) collective-permute-start(bf16[1,3,1024]{1,2,0:T(8,128)(2,1)} %copy.122), channel_id=1, source_target_pairs={{0,4},{4,8},{8,12},{1,5},{5,9},{9,13},{2,6},{6,10},{10,14},{3,7},{... | collective-permute-start | bytes 18440 | tf_op jit(solution)/shard_map/ppermute | solution.py:13
  31.0 1.5 copy.123
  32.9 13.7 %all_gather.22 = f32[4,1,16]{2,1,0:T(1,128)} all-gather(f32[1,1,16]{2,1,0:T(1,128)S(1)} %mul.357), channel_id=1, replica_groups=mesh['groups'=2,'seq'=4,'chan'=2,'dp'=2] {'seq'}, dimensions={0}, use_global_device_ids=true | all-gather | bytes 320 | tf_op jit(solution)/shard_map/all_gather | solution.py:20
  51.1 21.5 %all-gather.5.cloned.1.call-done = f32[64,64,128]{2,1,0:T(8,128)} async-done(((f32[16,64,128]{2,1,0:T(8,128)}), f32[64,64,128]{2,1,0:T(8,128)}) %all-gather.5.cloned.1.call-update) | async-done | bytes 2097168 | tf_op jit(solution)/shard_map/all_gather | solution.py:20
  72.6 5.5 %while.26 = (s32[]{:T(128)}, f32[1,16,64,128]{3,2,1,0:T(8,128)S(1)}, s32[]{:T(128)}, f32[4,1,16]{2,1,0:T(1,128)}, f32[4,1,16,64,128]{4,3,2,1,0:T(8,128)}, /*index=5*/s32[]{:T(128)}, s32[]{:T(128)}, s32[]{:T(128)}, s32[]{:T(128)}) while((s32[]{:T(128)}, f32[1,16,64,128]{3,2,1,0:T(8,128)S(1)}, s32[]{:T(128)}, f32[4,1,16]{2,1,0:T(1,128)}, ...), condition=%wide.region_10.11_spmd, body=%wide.region_9.10_spmd.sunk | while | flops 262150 | bytes 1573203 | solution.py:29
  73.2 1.2 bitcast_add_fusion.12
  75.0 1.2 bitcast_add_fusion.12
  79.8 1.3 fusion.34
  81.2 1.3 fusion.35
  82.6 6.2 %fusion.12 = (f32[1024]{0:T(1024)S(1)}, f32[1024]{0:T(1024)S(1)}, f32[1024]{0:T(1024)S(1)}, f32[1024]{0:T(1024)S(1)}, bf16[1,512,1024]{1,2,0:T(8,128)(2,1)}, /*index=5*/f32[1,512,1024]{1,2,0:T(8,128)S(1)}) fusion(bf16[1,512,1024]{1,2,0:T(8,128)(2,1)S(1)} %copy.123, bf16[1,3,1024]{1,2,0:T(8,128)(2,1)} %collective-permute-done, ...), kind=kLoop, calls=%fused_computation.35 | loop fusion | flops 25686016 | bytes 6363648 | tf_op jit(solution)/shard_map/reduce_sum | solution.py:202
  91.6 1.7 slice.175
  93.3 1.3 collective-permute-start.1
  94.6 27.7 %all_gather.27 = f32[8,4,1024]{2,1,0:T(4,128)S(1)} all-gather(f32[1,4,1024]{2,1,0:T(4,128)S(1)} %maximum_multiply_fusion), channel_id=1, replica_groups=mesh['groups'=2,'seq'=4,'chan'=2,'dp'=2] {'seq','dp'}, dimensions={0}, use_global_device_ids=true | all-gather | bytes 147456 | tf_op jit(solution)/shard_map/all_gather | solution.py:205
  122.9 1.5 convolution_bitcast_fusion.14
  124.4 1.6 convolution_bitcast_fusion.12
  126.7 1.6 convert_reduce_fusion.1
  130.1 1.6 convert_reduce_fusion
  132.6 6.0 %all-gather.7.cloned.1.call-done = f32[64,64,128]{2,1,0:T(8,128)} async-done(((f32[16,64,128]{2,1,0:T(8,128)}), f32[64,64,128]{2,1,0:T(8,128)}) %all-gather.7.cloned.1.call-update) | async-done | bytes 2097168 | tf_op jit(solution)/shard_map/all_gather | solution.py:20
  143.5 3.9 %fusion.11 = bf16[1,512,1024]{1,2,0:T(8,128)(2,1)S(1)} fusion(bf16[1,512,1024]{1,2,0:T(8,128)(2,1)S(1)} %copy-done, bf16[1,3,1024]{1,2,0:T(8,128)(2,1)} %collective-permute-done.1, f32[1024]{0:T(1024)S(1)} %bitcast.442, f32[1024]{0:T(1024)S(1)} %bitcast.444, f32[1024]{0:T(1024)S(1)} %bitcast.440, f32[1024]{0:T(1024)S(1)} %bitcast.438), kind=kLoop, calls=%fused_computation.34 | loop fusion | flops 11010048 | bytes 2119680 | tf_op jit(solution)/shard_map/convert_element_type | solution.py:105
  147.4 1.3 copy.126
  148.7 19.8 %all-reduce.3.cloned.1.call-done = (bf16[1,512,128]{2,1,0:T(8,128)(2,1)}, bf16[1,512,128]{2,1,0:T(8,128)(2,1)}) async-done(((bf16[1,512,128]{2,1,0:T(8,128)(2,1)}, bf16[1,512,128]{2,1,0:T(8,128)(2,1)}), (bf16[1,512,128]{2,1,0:T(8,128)(2,1)}, bf16[1,512,128]{2,1,0:T(8,128)(2,1)})) %all-reduce.3.cloned.1.call-update) | async-done | bytes 262160 | tf_op jit(solution)/shard_map/psum | solution.py:190
  168.4 1.6 convert_element_type.247
  170.1 1.6 convert_element_type.254
  (213 shorter events, 33.9 us)
Async XLA Ops:
  7.2 65.4 %all-gather.5.cloned.1.call-start = ((), (), s32[]{:S(2)}) async-start(), calls=%async_computation | async-start | bytes 2621440 | tf_op jit(solution)/shard_map/all_gather | solution.py:20
  13.6 4.9 %copy-start.33 = (s32[256]{0:T(256)}, s32[256]{0:T(256)S(1)}, u32[]{:S(2)}) copy-start(s32[256]{0:T(256)S(1)} %get-tuple-element.233) | copy-start | bytes 3076
  17.9 2.7 %copy-start.11 = (f32[1,256,16]{1,2,0:T(8,128)}, f32[1,256,16]{1,2,0:T(8,128)S(1)}, u32[]{:S(2)}) copy-start(f32[1,256,16]{1,2,0:T(8,128)S(1)} %copy.156) | copy-start | bytes 49156
  23.6 23.0 %copy-start.32 = (f32[4,1024]{1,0:T(4,128)S(1)}, f32[4,1024]{1,0:T(4,128)}, u32[]{:S(2)}) copy-start(f32[4,1024]{1,0:T(4,128)} %param.13) | copy-start | bytes 49156
  23.6 24.8 %copy-start.15 = (f32[1,512,16]{1,2,0:T(8,128)S(1)}, f32[1,512,16]{1,2,0:T(8,128)}, u32[]{:S(2)}) copy-start(f32[1,512,16]{1,2,0:T(8,128)} %param.14) | copy-start | bytes 98308
  23.6 24.8 %copy-start.38 = (pred[512]{0:T(512)(128)(4,1)S(1)}, pred[512]{0:T(512)(128)(4,1)}, u32[]{:S(2)}) copy-start(pred[512]{0:T(512)(128)(4,1)} %copy-done.37) | copy-start | bytes 1540
  23.6 24.8 %copy-start.34 = (s32[256]{0:T(256)S(1)}, s32[256]{0:T(256)}, u32[]{:S(2)}) copy-start(s32[256]{0:T(256)} %copy-done.33) | copy-start | bytes 3076
  23.6 25.6 %copy-start.36 = (s32[256]{0:T(256)S(1)}, s32[256]{0:T(256)}, u32[]{:S(2)}) copy-start(s32[256]{0:T(256)} %copy-done.35) | copy-start | bytes 3076
  23.6 25.7 %copy-start.3 = (bf16[1,512,128]{2,1,0:T(8,128)(2,1)S(1)}, bf16[1,512,128]{2,1,0:T(8,128)(2,1)}, u32[]{:S(2)}) copy-start(bf16[1,512,128]{2,1,0:T(8,128)(2,1)} %param.15) | copy-start | bytes 393220
  23.6 114.9 %all-gather.7.cloned.1.call-start = ((), (), s32[]{:S(2)}) async-start(), calls=%async_computation.1 | async-start | bytes 2621440 | tf_op jit(solution)/shard_map/all_gather | solution.py:20
  25.3 57.2 %collective-permute-start = (bf16[1,3,1024]{1,2,0:T(8,128)(2,1)}, bf16[1,3,1024]{1,2,0:T(8,128)(2,1)}, u32[]{:S(2)}, u32[]{:S(2)}) collective-permute-start(bf16[1,3,1024]{1,2,0:T(8,128)(2,1)} %copy.122), channel_id=1, source_target_pairs={{0,4},{4,8},{8,12},{1,5},{5,9},{9,13},{2,6},{6,10},{10,14},{3,7},{... | collective-permute-start | bytes 18440 | tf_op jit(solution)/shard_map/ppermute | solution.py:13
  32.8 57.3 %copy-start.7 = (f32[1,256,16]{1,2,0:T(8,128)}, f32[1,256,16]{1,2,0:T(8,128)S(1)}, u32[]{:S(2)}) copy-start(f32[1,256,16]{1,2,0:T(8,128)S(1)} %copy.157) | copy-start | bytes 49156
  49.3 31.8 %copy-start.16 = (pred[256,256]{1,0:T(8,128)(4,1)}, pred[256,256]{1,0:T(8,128)(4,1)S(1)}, u32[]{:S(2)}) copy-start(pred[256,256]{1,0:T(8,128)(4,1)S(1)} %fusion.110) | copy-start | bytes 196612
  72.6 5.8 %copy-start.41 = (f32[16]{0:T(128)S(1)}, f32[16]{0:T(128)}, u32[]{:S(2)}) copy-start(f32[16]{0:T(128)} %get-tuple-element.255) | copy-start | bytes 196
  91.6 76.9 %all-reduce.3.cloned.1.call-start = ((), (), s32[]{:S(2)}) async-start(), calls=%async_computation.2 | async-start | bytes 524288 | tf_op jit(solution)/shard_map/psum | solution.py:190
  93.3 50.1 %collective-permute-start.1 = (bf16[1,3,1024]{1,2,0:T(8,128)(2,1)}, bf16[1,3,1024]{1,2,0:T(8,128)(2,1)}, u32[]{:S(2)}, u32[]{:S(2)}) collective-permute-start(bf16[1,3,1024]{1,2,0:T(8,128)(2,1)} %slice.175), channel_id=1, source_target_pairs={{4,0},{8,4},{12,8},{5,1},{9,5},{13,9},{6,2},{10,6},{14,10},{7,3},{... | collective-permute-start | bytes 18440 | tf_op jit(solution)/shard_map/ppermute | solution.py:13
  122.9 3.1 %copy-start.2 = (f32[1,16,64,128]{3,2,1,0:T(8,128)S(1)}, f32[1,16,64,128]{3,2,1,0:T(8,128)}, u32[]{:S(2)}) copy-start(f32[1,16,64,128]{3,2,1,0:T(8,128)} %copy-done.1) | copy-start | bytes 1572868
  122.9 3.1 %copy-start.8 = (f32[1,256,16]{1,2,0:T(8,128)S(1)}, f32[1,256,16]{1,2,0:T(8,128)}, u32[]{:S(2)}) copy-start(f32[1,256,16]{1,2,0:T(8,128)} %copy-done.7) | copy-start | bytes 49156
  124.4 2.3 %copy-start.19 = (pred[256,256]{1,0:T(8,128)(4,1)S(1)}, pred[256,256]{1,0:T(8,128)(4,1)}, u32[]{:S(2)}) copy-start(pred[256,256]{1,0:T(8,128)(4,1)} %fusion.111) | copy-start | bytes 196612
  124.4 2.3 %copy-start.31 = (f32[16,256]{1,0:T(8,128)S(1)}, f32[16,256]{1,0:T(8,128)}, u32[]{:S(2)}) copy-start(f32[16,256]{1,0:T(8,128)} %bitcast_add_fusion.5) | copy-start | bytes 49156
  131.7 6.9 %copy-start.5 = (bf16[256,256]{1,0:T(8,128)(2,1)}, bf16[256,256]{1,0:T(8,128)(2,1)S(1)}, u32[]{:S(2)}) copy-start(bf16[256,256]{1,0:T(8,128)(2,1)S(1)} %convert_reduce_fusion) | copy-start | bytes 393220
  141.6 1.8 %copy-start = (bf16[1,512,1024]{1,2,0:T(8,128)(2,1)S(1)}, bf16[1,512,1024]{1,2,0:T(8,128)(2,1)}, u32[]{:S(2)}) copy-start(bf16[1,512,1024]{1,2,0:T(8,128)(2,1)} %get-tuple-element.228) | copy-start | bytes 3145732
  141.6 1.8 %copy-start.21 = (f32[1,1024]{1,0:T(1,128)S(1)}, f32[1,1024]{1,0:T(1,128)}, u32[]{:S(2)}) copy-start(f32[1,1024]{1,0:T(1,128)} %get-tuple-element.244) | copy-start | bytes 12292
  141.6 1.8 %copy-start.23 = (f32[1,1024]{1,0:T(1,128)S(1)}, f32[1,1024]{1,0:T(1,128)}, u32[]{:S(2)}) copy-start(f32[1,1024]{1,0:T(1,128)} %get-tuple-element.245) | copy-start | bytes 12292
  (27 other events, 32.5 us)
Sparse Core Ops, SparseCore 0:
  23.7 48.7 all-gather.4
  91.7 46.8 all-gather.6
  143.5 24.8 all-reduce.2
